TPU v7x, 256 devices: a whole 4x4x8 slice. The times are simulated.
256 devices in a mesh: dp: 8 (over x, y_hi), tm: 2 (over y_lo), space: 16 (over z, core).
Axes of the slice: x: 4, y: 4 (y_hi: 2, y_lo: 2; y = y_hi * 2 + y_lo), z: 8, core: 2. Of those that a mesh axis runs over, the one named last changes fastest.
Arguments:
- latents: bfloat16 [256, 4, 256, 512], P(('dp', 'tm', 'space')), parts along dimension 0, may hold values from -36 to 36, as said below
- norm_gain: float32 [512], replicated, may hold values from 0.1 to 1.9
- conv_weight: bfloat16 [3, 3, 3, 512, 256], replicated, may hold values from -0.0546875 to 0.0546875
- skip_weight: bfloat16 [512, 256], replicated, may hold values from -0.25 to 0.25
- cotangent: bfloat16 [256, 16, 4, 16, 256], P(('dp', 'tm'), 'space'), parts along dimension 0, may hold values from -6 to 6
Outputs:
- output: bfloat16 [256, 16, 4, 16, 256], P(('dp', 'tm'), 'space'), parts along dimension 0
- grad_input: bfloat16 [256, 16, 4, 16, 512], P(('dp', 'tm'), 'space'), parts along dimension 0
There are 8 independent parts, one for each index of `dp`. A program takes and returns all parts, laid end to end along the dimension named above; an argument that names none is the same for every part. Nothing has to cross between parts.
Inputs may be any that keep to these rules, and one draw needn't show every extreme that they name: `latents`: each cell and each channel has its own scale.
All inputs are finite; a program needn't handle non-finite values.
Results may differ from a plain program's by a relative error of at most 0.002.
Values may be sent and summed in bfloat16 or wider, within the bound.
A program may use at most 192 MiB of HBM per device.

v0:
```python
import jax
import jax.numpy as jnp
from jax import lax
from jax.sharding import PartitionSpec as P

epsilon = 1e-06


def extended_2(block, sides, width):
    for axis, dim in sides:
        count = lax.axis_size(axis)
        forward = [(i, i + 1) for i in range(count - 1)]
        backward = [(target, source) for source, target in forward]
        low = lax.ppermute(
            lax.slice_in_dim(block, block.shape[dim] - width, None, axis=dim), axis, forward
        )
        high = lax.ppermute(lax.slice_in_dim(block, 0, width, axis=dim), axis, backward)
        block = jnp.concatenate([low, block, high], axis=dim)
    return block


def shifted(value, axis, steps):
    count = lax.axis_size(axis)
    first, last = (max(0, -steps), min(count, count - steps))
    return lax.ppermute(value, axis, [(source, source + steps) for source in range(first, last)])


def activate(x_float, norm_gain):
    mean_sq = jnp.mean(x_float * x_float, axis=-1, keepdims=True)
    inv_rms = lax.rsqrt(mean_sq + epsilon)
    unit_val = x_float * inv_rms
    return (inv_rms, unit_val, unit_val * norm_gain)


def silu_slope(normed):
    sigma_val = jax.nn.sigmoid(normed)
    return sigma_val * (1.0 + normed * (1.0 - sigma_val))


def spread(field):
    widened = extended_2(field, (("space", 2),), 1)
    return jnp.pad(widened, ((0, 0), (1, 1), (0, 0), (0, 0)))


def local(latents, norm_gain, conv_weight, skip_weight, cotangent):
    strips = lax.axis_size("space")
    frame_count, height, width, in_chan = latents.shape
    group_len, single, tile_rows, tile_cols, out_chan = cotangent.shape
    outgoing = latents.reshape(frame_count, height, strips, tile_cols, in_chan).transpose(
        2, 0, 1, 3, 4
    )
    arrived = lax.all_to_all(outgoing, "space", split_axis=0, concat_axis=1, tiled=True)[0]
    inv_rms, unit_val, normed = activate(arrived.astype(jnp.float32), norm_gain)
    hidden = jax.nn.silu(normed).astype(jnp.bfloat16)
    hidden_pad = spread(hidden)
    past_rows = shifted(hidden_pad[group_len - 2 :], "tm", 1)
    extended = jnp.concatenate([past_rows, hidden_pad], 0)
    summed = jnp.dot(arrived.reshape(-1, in_chan), skip_weight, preferred_element_type=jnp.float32)
    for t_tap in range(3):
        for h_tap in range(3):
            for w_tap in range(3):
                window = extended[
                    t_tap : t_tap + group_len, h_tap : h_tap + tile_rows, w_tap : w_tap + tile_cols
                ]
                summed = summed + jnp.dot(
                    window.reshape(-1, in_chan),
                    conv_weight[t_tap, h_tap, w_tap],
                    preferred_element_type=jnp.float32,
                )
    output = summed.astype(jnp.bfloat16).reshape(group_len, 1, tile_rows, tile_cols, out_chan)
    grad_out = cotangent[:, 0]
    grad_pad = spread(grad_out)
    next_rows = shifted(grad_pad[0:2], "tm", -1)
    grad_ext = jnp.concatenate([grad_pad, next_rows], 0)
    contract = (((1,), (1,)), ((), ()))
    grad_skip = lax.dot_general(
        grad_out.reshape(-1, out_chan), skip_weight, contract, preferred_element_type=jnp.float32
    )
    grad_hidden = jnp.zeros((group_len * tile_rows * tile_cols, in_chan), jnp.float32)
    for t_tap in range(3):
        for h_tap in range(3):
            for w_tap in range(3):
                window = grad_ext[
                    2 - t_tap : 2 - t_tap + group_len,
                    2 - h_tap : 2 - h_tap + tile_rows,
                    2 - w_tap : 2 - w_tap + tile_cols,
                ]
                grad_hidden = grad_hidden + lax.dot_general(
                    window.reshape(-1, out_chan),
                    conv_weight[t_tap, h_tap, w_tap],
                    contract,
                    preferred_element_type=jnp.float32,
                )
    grad_unit = (
        grad_hidden.reshape(group_len, tile_rows, tile_cols, in_chan)
        * silu_slope(normed)
        * norm_gain
    )
    grad_input = inv_rms * (
        grad_unit - unit_val * jnp.mean(grad_unit * unit_val, axis=-1, keepdims=True)
    )
    grad_input = grad_input + grad_skip.reshape(group_len, tile_rows, tile_cols, in_chan)
    return (
        output,
        grad_input.astype(jnp.bfloat16).reshape(group_len, 1, tile_rows, tile_cols, in_chan),
    )


def solution(mesh):
    placed = (
        P(("dp", "tm", "space"), None, None, None),
        P(),
        P(),
        P(),
        P(("dp", "tm"), "space", None, None, None),
    )
    return jax.shard_map(
        local,
        mesh=mesh,
        in_specs=placed,
        out_specs=(
            P(("dp", "tm"), "space", None, None, None),
            P(("dp", "tm"), "space", None, None, None),
        ),
        check_vma=False,
    )
```

profile of v0, /device:TPU:125, one launch (start us, length us, event | category | flops | bytes accessed | tf_op | source)
XLA Modules:
  0.0 144.2 jit_solution(12745354876718055685)
XLA Ops:
  0.6 1.8 %fusion.262 = (bf16[16,4,1,256]{3,2,1,0:T(2,128)(2,1)}, bf16[16,4,1,256]{3,2,1,0:T(2,128)(2,1)}) fusion(bf16[16,4,16,256]{3,2,1,0:T(8,128)(2,1)} %bitcast.326), kind=kLoop, calls=%fused_computation.315 | loop fusion | bytes 131072 | tf_op jit(solution)/shard_map/slice | solution.py:15
  2.5 5.3 %collective-permute-start.3 = (bf16[16,4,1,256]{3,2,1,0:T(2,128)(2,1)}, bf16[16,4,1,256]{3,2,1,0:T(2,128)(2,1)S(1)}, u32[]{:S(2)}, u32[]{:S(2)}) collective-permute-start(bf16[16,4,1,256]{3,2,1,0:T(2,128)(2,1)} %get-tuple-element.62), channel_id=1, source_target_pairs={{0,1},{1,2},{2,3},{3,4},{4,5},{5,6},{6,7},{7,8},{8,9},{9,10},{10,1... | collective-permute-start | bytes 98312 | tf_op jit(solution)/shard_map/ppermute | solution.py:14
  7.8 1.9 %collective-permute-start.4 = (bf16[16,4,1,256]{3,2,1,0:T(2,128)(2,1)}, bf16[16,4,1,256]{3,2,1,0:T(2,128)(2,1)S(1)}, u32[]{:S(2)}, u32[]{:S(2)}) collective-permute-start(bf16[16,4,1,256]{3,2,1,0:T(2,128)(2,1)} %get-tuple-element.63), channel_id=1, source_target_pairs={{1,0},{2,1},{3,2},{4,3},{5,4},{6,5},{7,6},{8,7},{9,8},{10,9},{11,1... | collective-permute-start | bytes 98312 | tf_op jit(solution)/shard_map/ppermute | solution.py:17
  9.7 2.3 %copy.12 = bf16[16,1,4,16,512]{4,3,2,1,0:T(8,128)(2,1)} copy(bf16[16,1,4,16,512]{4,3,0,2,1:T(8,128)(2,1)} %bitcast.384) | data formatting | bytes 2097152 | tf_op jit(solution)/shard_map/transpose | solution.py:49
  12.0 7.5 %all-to-all-start = ((bf16[16,1,4,16,512]{4,3,2,1,0:T(8,128)(2,1)}), bf16[16,1,4,16,512]{4,3,2,1,0:T(8,128)(2,1)S(1)}, u32[]{:S(2)}, u32[]{:S(2)}) async-start(bf16[16,1,4,16,512]{4,3,2,1,0:T(8,128)(2,1)} %copy.12), calls=%async_computation | async-start | bytes 2097152 | tf_op jit(solution)/shard_map/all_to_all | solution.py:52
  21.3 2.0 %fusion.64 = bf16[16,6,18,256]{3,2,1,0:T(8,128)(2,1)S(1)} fusion(bf16[16,4,1,256]{3,2,1,0:T(2,128)(2,1)S(1)} %collective-permute-done.4, bf16[16,4,16,256]{3,2,1,0:T(8,128)(2,1)} %bitcast.328, bf16[16,4,1,256]{3,2,1,0:T(2,128)(2,1)S(1)} %collective-permute-done.3), kind=kLoop, calls=%fused_computation.109 | loop fusion | flops 5308416 | bytes 1474560 | tf_op jit(solution)/shard_map/concatenate | solution.py:18
  23.5 2.4 %collective-permute-start.5 = (bf16[2,6,18,256]{3,2,1,0:T(8,128)(2,1)S(1)}, bf16[2,6,18,256]{3,2,1,0:T(8,128)(2,1)S(1)}, u32[]{:S(2)}, u32[]{:S(2)}) collective-permute-start(bf16[2,6,18,256]{3,2,1,0:T(8,128)(2,1)S(1)} %slice.424), channel_id=1, source_target_pairs={{16,0},{17,1},{18,2},{19,3},{20,4},{21,5},{22,6},{23,7},{24,8},{25... | collective-permute-start | bytes 331784 | tf_op jit(solution)/shard_map/ppermute | solution.py:25
  33.8 1.9 %fusion.122 = f32[1024,512]{1,0:T(8,128)} fusion(bf16[1024,256]{1,0:T(8,128)(2,1)S(1)} %bitcast.366, bf16[3,3,3,512,256]{4,3,2,1,0:T(8,128)(2,1)S(1)} %copy-done.2), kind=kOutput, calls=%fused_computation.173 | convolution fusion | flops 268435456 | bytes 2883584 | tf_op jit(solution)/shard_map/dot_general | solution.py:88
  35.7 1.9 %fusion.126 = f32[1024,512]{1,0:T(8,128)} fusion(bf16[1024,256]{1,0:T(8,128)(2,1)S(1)} %bitcast.365, bf16[3,3,3,512,256]{4,3,2,1,0:T(8,128)(2,1)S(1)} %copy-done.2), kind=kOutput, calls=%fused_computation.177 | convolution fusion | flops 268435456 | bytes 2883584 | tf_op jit(solution)/shard_map/dot_general | solution.py:88
  46.5 1.9 %fusion.154 = f32[1024,512]{1,0:T(8,128)} fusion(bf16[1024,256]{1,0:T(8,128)(2,1)S(1)} %bitcast.359, bf16[3,3,3,512,256]{4,3,2,1,0:T(8,128)(2,1)S(1)} %copy-done.2), kind=kOutput, calls=%fused_computation.205 | convolution fusion | flops 268435456 | bytes 2883584 | tf_op jit(solution)/shard_map/dot_general | solution.py:88
  53.4 1.9 %fusion.158 = f32[1024,512]{1,0:T(8,128)} fusion(bf16[1024,256]{1,0:T(8,128)(2,1)S(1)} %bitcast.381, bf16[3,3,3,512,256]{4,3,2,1,0:T(8,128)(2,1)S(1)} %copy-done.2), kind=kOutput, calls=%fused_computation.209 | convolution fusion | flops 268435456 | bytes 2883584 | tf_op jit(solution)/shard_map/dot_general | solution.py:88
  62.4 1.8 %fusion.178 = f32[1024,512]{1,0:T(8,128)} fusion(bf16[1024,256]{1,0:T(8,128)(2,1)S(1)} %bitcast.376, bf16[3,3,3,512,256]{4,3,2,1,0:T(8,128)(2,1)S(1)} %copy-done.2), kind=kOutput, calls=%fused_computation.229 | convolution fusion | flops 268435456 | bytes 2883584 | tf_op jit(solution)/shard_map/dot_general | solution.py:88
  66.0 1.8 %fusion.186 = f32[1024,512]{1,0:T(8,128)} fusion(bf16[1024,256]{1,0:T(8,128)(2,1)S(1)} %bitcast.374, bf16[3,3,3,512,256]{4,3,2,1,0:T(8,128)(2,1)S(1)} %copy-done.2), kind=kOutput, calls=%fused_computation.237 | convolution fusion | flops 268435456 | bytes 2883584 | tf_op jit(solution)/shard_map/dot_general | solution.py:88
  67.9 1.8 %fusion.190 = f32[1024,512]{1,0:T(8,128)} fusion(bf16[1024,256]{1,0:T(8,128)(2,1)S(1)} %bitcast.373, bf16[3,3,3,512,256]{4,3,2,1,0:T(8,128)(2,1)S(1)} %copy-done.2), kind=kOutput, calls=%fused_computation.241 | convolution fusion | flops 268435456 | bytes 2883584 | tf_op jit(solution)/shard_map/dot_general | solution.py:88
  75.5 19.4 %multiply_reduce_fusion = (f32[1024]{0:T(1024)S(1)}, f32[1024,512]{1,0:T(8,128)}) fusion(f32[512]{0:T(512)S(1)} %copy-done.7, f32[1024]{0:T(1024)S(1)} %rsqrt.13, bf16[16,1,4,16,512]{4,3,2,1,0:T(8,128)(2,1)S(1)} %all-to-all-done, f32[1024,512]{1,0:T(8,128)} %fusion.100, f32[1024,512]{1,0:T(8,128)} %fusion.104, f32[1024,512]{1,0:T(8,128)} %fusion.108, ...), kind=kOutput, calls=%fused_computation.74 | convolution fusion | flops 289405952 | bytes 58468352 | tf_op jit(solution)/shard_map/dot_general | solution.py:88
  95.8 4.8 %collective-permute-start = (bf16[16,4,1,512]{3,2,1,0:T(2,128)(2,1)S(1)}, bf16[16,4,1,512]{3,2,1,0:T(2,128)(2,1)S(1)}, u32[]{:S(2)}, u32[]{:S(2)}) collective-permute-start(bf16[16,4,1,512]{3,2,1,0:T(2,128)(2,1)S(1)} %get-tuple-element.58), channel_id=1, source_target_pairs={{0,1},{1,2},{2,3},{3,4},{4,5},{5,6},{6,7},{7,8},{8,9},{9,10},{10,1... | collective-permute-start | bytes 196616 | tf_op jit(solution)/shard_map/ppermute | solution.py:14
  100.7 1.9 %collective-permute-start.1 = (bf16[16,4,1,512]{3,2,1,0:T(2,128)(2,1)S(1)}, bf16[16,4,1,512]{3,2,1,0:T(2,128)(2,1)S(1)}, u32[]{:S(2)}, u32[]{:S(2)}) collective-permute-start(bf16[16,4,1,512]{3,2,1,0:T(2,128)(2,1)S(1)} %get-tuple-element.59), channel_id=1, source_target_pairs={{1,0},{2,1},{3,2},{4,3},{5,4},{6,5},{7,6},{8,7},{9,8},{10,9},{11,1... | collective-permute-start | bytes 196616 | tf_op jit(solution)/shard_map/ppermute | solution.py:17
  104.8 2.4 %fusion.34 = bf16[16,1,4,16,512]{4,3,2,1,0:T(8,128)(2,1)} fusion(f32[16,4,16,512]{3,2,1,0:T(8,128)S(1)} %bitcast.358, bf16[16,1,4,16,512]{4,3,2,1,0:T(8,128)(2,1)S(1)} %all-to-all-done, f32[16,4,16]{2,1,0:T(4,128)S(1)} %div.25, f32[512]{0:T(512)S(1)} %copy-done.7, f32[16,4,16]{2,1,0:T(4,128)S(1)} %add_rsqrt_fusion, bf16[512,256]{1,0:T(8,128)(2,1)S(1)} %copy-done, ...), kind=kOutput, calls=%fused_computation.76 | convolution fusion | flops 277348352 | bytes 4990976 | tf_op jit(solution)/shard_map/dot_general | solution.py:76
  111.5 2.1 %pad_maximum_fusion = (bf16[16,4,16,512]{3,2,1,0:T(8,128)(2,1)}, bf16[16,4,16,512]{3,2,1,0:T(8,128)(2,1)S(1)}) fusion(bf16[16,4,1,512]{3,2,1,0:T(2,128)(2,1)S(1)} %collective-permute-done.1, bf16[16,4,16,512]{3,2,1,0:T(8,128)(2,1)S(1)} %fusion.17, bf16[16,4,1,512]{3,2,1,0:T(2,128)(2,1)S(1)} %collective-permute-done), kind=kLoop, calls=%fused_computation.127 | loop fusion | flops 4194304 | bytes 3276800 | tf_op jit(solution)/shard_map/concatenate | solution.py:18
  115.5 4.6 %collective-permute-done.2 = bf16[2,6,18,512]{3,2,1,0:T(8,128)(2,1)S(1)} collective-permute-done((bf16[2,6,18,512]{3,2,1,0:T(8,128)(2,1)S(1)}, bf16[2,6,18,512]{3,2,1,0:T(8,128)(2,1)S(1)}, u32[]{:S(2)}, u32[]{:S(2)}) %collective-permute-start.2) | collective-permute-done | bytes 221216 | tf_op jit(solution)/shard_map/ppermute | solution.py:25
  120.1 2.1 %fusion.78 = (bf16[16,4,16,512]{3,2,1,0:T(8,128)(2,1)S(1)}, bf16[16,4,16,512]{3,2,1,0:T(8,128)(2,1)S(1)}, bf16[16,4,16,512]{3,2,1,0:T(8,128)(2,1)S(1)}, bf16[16,...) fusion(bf16[2,6,18,512]{3,2,1,0:T(8,128)(2,1)S(1)} %collective-, ...), kind=kLoop, calls=%fused_computation.123 | loop fusion | flops 12582912 | bytes 13139968 | tf_op jit(solution)/shard_map/concatenate | solution.py:57
  129.6 2.3 %fusion.67 = (bf16[16,4,16,512]{3,2,1,0:T(8,128)(2,1)}, bf16[16,4,16,512]{3,2,1,0:T(8,128)(2,1)S(1)}, bf16[16,4,16,512]{3,2,1,0:T(8,128)(2,1)S(1)}, bf16[16,4,16...) fusion(bf16[2,6,18,512]{3,2,1,0:T(8,128)(2,1)S(1)} %collective-, ...), kind=kLoop, calls=%fused_computation.112 | loop fusion | flops 3145728 | bytes 11042816 | tf_op jit(solution)/shard_map/concatenate | solution.py:57
  136.9 3.5 %fusion.61 = f32[1024,256]{1,0:T(8,128)} fusion(f32[1024,256]{1,0:T(8,128)S(1)} %fusion.116, f32[1024,256]{1,0:T(8,128)S(1)} %fusion.120, f32[1024,256]{1,0:T(8,128)S(1)} %fusion.124, f32[1024,256]{1,0:T(8,128)S(1)} %fusion.128, f32[1024,256]{1,0:T(8,128)S(1)} %fusion.132, f32[1024,256]{1,0:T(8,128)S(1)} %fusion.136, f32[1024,256]{1,0:T(8,128)S(1)} %fusion.140, ...), kind=kOutput, calls=%fused_computation.106 | convolution fusion | flops 274202624 | bytes 25427968 | tf_op jit(solution)/shard_map/dot_general | solution.py:65
  140.4 3.8 %fusion.62 = bf16[1024,256]{1,0:T(8,128)(2,1)} fusion(f32[1024,256]{1,0:T(8,128)} %fusion.102, f32[1024,256]{1,0:T(8,128)} %fusion.106, f32[1024,256]{1,0:T(8,128)} %fusion.110, f32[1024,256]{1,0:T(8,128)} %fusion.61, bf16[1024,512]{1,0:T(8,128)(2,1)} %bitcast.340, bf16[3,3,3,512,256]{4,3,2,1,0:T(8,128)(2,1)S(1)} %bitcast.325), kind=kOutput, calls=%fused_computation.107 | convolution fusion | flops 269746176 | bytes 6029312 | tf_op jit(solution)/shard_map/dot_general | solution.py:65
  (91 shorter events, 60.1 us)
Async XLA Ops:
  0.6 102.0 %copy-start = (bf16[512,256]{1,0:T(8,128)(2,1)S(1)}, bf16[512,256]{1,0:T(8,128)(2,1)}, u32[]{:S(2)}) copy-start(bf16[512,256]{1,0:T(8,128)(2,1)} %param.8) | copy-start | bytes 786436
  2.5 18.8 %collective-permute-start.3 = (bf16[16,4,1,256]{3,2,1,0:T(2,128)(2,1)}, bf16[16,4,1,256]{3,2,1,0:T(2,128)(2,1)S(1)}, u32[]{:S(2)}, u32[]{:S(2)}) collective-permute-start(bf16[16,4,1,256]{3,2,1,0:T(2,128)(2,1)} %get-tuple-element.62), channel_id=1, source_target_pairs={{0,1},{1,2},{2,3},{3,4},{4,5},{5,6},{6,7},{7,8},{8,9},{9,10},{10,1... | collective-permute-start | bytes 98312 | tf_op jit(solution)/shard_map/ppermute | solution.py:14
  7.8 13.5 %collective-permute-start.4 = (bf16[16,4,1,256]{3,2,1,0:T(2,128)(2,1)}, bf16[16,4,1,256]{3,2,1,0:T(2,128)(2,1)S(1)}, u32[]{:S(2)}, u32[]{:S(2)}) collective-permute-start(bf16[16,4,1,256]{3,2,1,0:T(2,128)(2,1)} %get-tuple-element.63), channel_id=1, source_target_pairs={{1,0},{2,1},{3,2},{4,3},{5,4},{6,5},{7,6},{8,7},{9,8},{10,9},{11,1... | collective-permute-start | bytes 98312 | tf_op jit(solution)/shard_map/ppermute | solution.py:17
  12.0 63.1 %all-to-all-start = ((bf16[16,1,4,16,512]{4,3,2,1,0:T(8,128)(2,1)}), bf16[16,1,4,16,512]{4,3,2,1,0:T(8,128)(2,1)S(1)}, u32[]{:S(2)}, u32[]{:S(2)}) async-start(bf16[16,1,4,16,512]{4,3,2,1,0:T(8,128)(2,1)} %copy.12), calls=%async_computation | async-start | bytes 2097152 | tf_op jit(solution)/shard_map/all_to_all | solution.py:52
  19.5 6.4 %copy-start.2 = (bf16[3,3,3,512,256]{4,3,2,1,0:T(8,128)(2,1)S(1)}, bf16[3,3,3,512,256]{4,3,2,1,0:T(8,128)(2,1)}, u32[]{:S(2)}) copy-start(bf16[3,3,3,512,256]{4,3,2,1,0:T(8,128)(2,1)} %param.7) | copy-start | bytes 21233668
  23.5 9.1 %collective-permute-start.5 = (bf16[2,6,18,256]{3,2,1,0:T(8,128)(2,1)S(1)}, bf16[2,6,18,256]{3,2,1,0:T(8,128)(2,1)S(1)}, u32[]{:S(2)}, u32[]{:S(2)}) collective-permute-start(bf16[2,6,18,256]{3,2,1,0:T(8,128)(2,1)S(1)} %slice.424), channel_id=1, source_target_pairs={{16,0},{17,1},{18,2},{19,3},{20,4},{21,5},{22,6},{23,7},{24,8},{25... | collective-permute-start | bytes 331784 | tf_op jit(solution)/shard_map/ppermute | solution.py:25
  27.7 1.8 %copy-start.3 = (bf16[16,1,4,16,256]{4,3,2,1,0:T(8,128)(2,1)S(1)}, bf16[16,1,4,16,256]{4,3,2,1,0:T(8,128)(2,1)}, u32[]{:S(2)}) copy-start(bf16[16,1,4,16,256]{4,3,2,1,0:T(8,128)(2,1)} %param.9) | copy-start | bytes 1572868
  73.3 2.2 %copy-start.7 = (f32[512]{0:T(512)S(1)}, f32[512]{0:T(512)}, u32[]{:S(2)}) copy-start(f32[512]{0:T(512)} %param.6) | copy-start | bytes 6148
  95.8 12.0 %collective-permute-start = (bf16[16,4,1,512]{3,2,1,0:T(2,128)(2,1)S(1)}, bf16[16,4,1,512]{3,2,1,0:T(2,128)(2,1)S(1)}, u32[]{:S(2)}, u32[]{:S(2)}) collective-permute-start(bf16[16,4,1,512]{3,2,1,0:T(2,128)(2,1)S(1)} %get-tuple-element.58), channel_id=1, source_target_pairs={{0,1},{1,2},{2,3},{3,4},{4,5},{5,6},{6,7},{7,8},{8,9},{9,10},{10,1... | collective-permute-start | bytes 196616 | tf_op jit(solution)/shard_map/ppermute | solution.py:14
  100.7 7.5 %collective-permute-start.1 = (bf16[16,4,1,512]{3,2,1,0:T(2,128)(2,1)S(1)}, bf16[16,4,1,512]{3,2,1,0:T(2,128)(2,1)S(1)}, u32[]{:S(2)}, u32[]{:S(2)}) collective-permute-start(bf16[16,4,1,512]{3,2,1,0:T(2,128)(2,1)S(1)} %get-tuple-element.59), channel_id=1, source_target_pairs={{1,0},{2,1},{3,2},{4,3},{5,4},{6,5},{7,6},{8,7},{9,8},{10,9},{11,1... | collective-permute-start | bytes 196616 | tf_op jit(solution)/shard_map/ppermute | solution.py:17
  102.6 2.1 %copy-start.4 = (bf16[16,1,4,16,256]{4,3,2,1,0:T(8,128)(2,1)S(1)}, bf16[16,1,4,16,256]{4,3,2,1,0:T(8,128)(2,1)}, u32[]{:S(2)}) copy-start(bf16[16,1,4,16,256]{4,3,2,1,0:T(8,128)(2,1)} %param.9) | copy-start | bytes 1572868
  102.6 2.1 %copy-start.6 = (f32[1024,512]{1,0:T(8,128)S(1)}, f32[1024,512]{1,0:T(8,128)}, u32[]{:S(2)}) copy-start(f32[1024,512]{1,0:T(8,128)} %get-tuple-element.65) | copy-start | bytes 6291460
  104.1 3.1 %slice-start = ((s8[7077888]{0:T(1024)(128)(4,1)}), s8[4194304]{0:T(1024)(128)(4,1)S(1)}, s32[]{:S(2)}) async-start(s8[7077888]{0:T(1024)(128)(4,1)} %bitcast.324), calls=%async_computation.1 | async-start | bytes 8388608
  104.8 2.7 %slice-start.1 = ((s8[7077888]{0:T(1024)(128)(4,1)}), s8[2883584]{0:T(1024)(128)(4,1)S(1)}, s32[]{:S(2)}) async-start(s8[7077888]{0:T(1024)(128)(4,1)} %bitcast.324), calls=%async_computation.2 | async-start | bytes 5767168
  109.8 10.3 %collective-permute-start.2 = (bf16[2,6,18,512]{3,2,1,0:T(8,128)(2,1)S(1)}, bf16[2,6,18,512]{3,2,1,0:T(8,128)(2,1)S(1)}, u32[]{:S(2)}, u32[]{:S(2)}) collective-permute-start(bf16[2,6,18,512]{3,2,1,0:T(8,128)(2,1)S(1)} %slice.381), channel_id=1, source_target_pairs={{0,16},{1,17},{2,18},{3,19},{4,20},{5,21},{6,22},{7,23},{8,24},{9,... | collective-permute-start | bytes 663560 | tf_op jit(solution)/shard_map/ppermute | solution.py:25
  133.7 2.8 %copy-start.5 = (f32[1024,256]{1,0:T(8,128)S(1)}, f32[1024,256]{1,0:T(8,128)}, u32[]{:S(2)}) copy-start(f32[1024,256]{1,0:T(8,128)} %fusion.263) | copy-start | bytes 3145732
  140.4 3.8 %copy-start.1 = (bf16[512,256]{1,0:T(8,128)(2,1)S(1)}, bf16[512,256]{1,0:T(8,128)(2,1)}, u32[]{:S(2)}) copy-start(bf16[512,256]{1,0:T(8,128)(2,1)} %param.8) | copy-start | bytes 786436
where the time goes:
time: 145 us; the launch traced here: 144 us
  matrix products  91 us (63%)
  starting transfers between devices  25.2 us (17%)
  other arithmetic  16.4 us (11%)
  local copies, waits for them, and re-layouts  5.65 us (4%)
  waiting for transfers between devices  4.9 us (3%)
    dot_general x27, matrix products, local(): lax.dot_general(window.reshape(-1, out_chan), conv_weight[t_tap, h_tap, w...  66.2 us
    dot_general x27, matrix products, local(): jnp.dot(window.reshape(-1, in_chan), conv_weight[t_tap, h_tap, w_tap], pr...  21 us
    ppermute x2, starting transfers between devices, extended_2(): lax.ppermute(lax.slice_in_dim(block, block.shape[dim] - width, None, axis...  10.1 us
    all_to_all x1, starting transfers between devices, local(): lax.all_to_all(outgoing, 'space', split_axis=0, concat_axis=1, tiled=True)  7.53 us
    concatenate x4, other arithmetic, extended_2(): block = jnp.concatenate([low, block, high], axis=dim)  6.4 us
    concatenate x3, other arithmetic, local(): extended = jnp.concatenate([past_rows, hidden_pad], 0)  5.66 us
    ppermute x2, waiting for transfers between devices, shifted(): lax.ppermute(value, axis, [(source, source + steps) for source in range(f...  4.59 us
    ppermute x2, starting transfers between devices, extended_2(): lax.ppermute(lax.slice_in_dim(block, 0, width, axis=dim), axis, backward)  3.84 us
  transfers between devices with their start and end apart: 7, of which 2 were waited for; matrix products, arithmetic and copies ran while one was open for 45% of the time, Pallas kernels for 0%

commit v1 on v0

--- a/solution.py
+++ b/solution.py
@@ -49,7 +49,12 @@
     outgoing = latents.reshape(frame_count, height, strips, tile_cols, in_chan).transpose(
         2, 0, 1, 3, 4
     )
-    arrived = lax.all_to_all(outgoing, "space", split_axis=0, concat_axis=1, tiled=True)[0]
+    arrived = jnp.concatenate(
+        lax.all_to_all(
+            jnp.stack(jnp.split(outgoing, lax.axis_size("space"), axis=0)), "space", 0, 0
+        ),
+        axis=1,
+    )[0]
     inv_rms, unit_val, normed = activate(arrived.astype(jnp.float32), norm_gain)
     hidden = jax.nn.silu(normed).astype(jnp.bfloat16)
     hidden_pad = spread(hidden)

time: 145 us -> 181 us (1.25)
  local copies, waits for them, and re-layouts: 5.65 us -> 26.3 us
  waiting for transfers between devices: 4.9 us -> 22.2 us
  starting transfers between devices: 25.2 us -> 23.1 us
    unnamed x20 -> x35, local copies, waits for them, and re-layouts: 0.31 us -> 22.4 us
    ppermute x2, waiting for transfers between devices: 0.01 us -> 14.5 us  [extended_2(): lax.ppermute(lax.slice_in_dim(block, block.shape[dim] - width, None, axis...]
    ppermute x2, waiting for transfers between devices: 0.3 us -> 3.14 us  [extended_2(): lax.ppermute(lax.slice_in_dim(block, 0, width, axis=dim), axis, backward)]
    ppermute x2, starting transfers between devices: 10.1 us -> 7.62 us  [extended_2(): lax.ppermute(lax.slice_in_dim(block, block.shape[dim] - width, None, axis...]
    transpose x1 -> x0, local copies, waits for them, and re-layouts: 2.29 us -> none  [local(): latents.reshape(frame_count, height, strips, tile_cols, in_chan)]
  transfers between devices with their start and end apart: 7 -> 7, of which waited for: 2 -> 4; matrix products, arithmetic and copies ran while one was open for 45% -> 35% of each run, Pallas kernels for 0% -> 0%
where the time goes in v1:
time: 181 us; the launch traced here: 180 us
  matrix products  91 us (50%)
  local copies, waits for them, and re-layouts  26.3 us (15%)
  starting transfers between devices  23.1 us (13%)
  waiting for transfers between devices  22.2 us (12%)
  other arithmetic  16 us (9%)
    dot_general x27, matrix products, local(): lax.dot_general(window.reshape(-1, out_chan), conv_weight[t_tap, h_tap, w...  66.2 us
    unnamed x35, local copies, waits for them, and re-layouts  22.4 us
    dot_general x27, matrix products, local(): jnp.dot(window.reshape(-1, in_chan), conv_weight[t_tap, h_tap, w_tap], pr...  21 us
    ppermute x2, waiting for transfers between devices, extended_2(): lax.ppermute(lax.slice_in_dim(block, block.shape[dim] - width, None, axis...  14.5 us
    all_to_all x1, starting transfers between devices, local(): lax.all_to_all(jnp.stack(jnp.split(outgoing, lax.axis_size('space'), axis...  7.99 us
    ppermute x2, starting transfers between devices, extended_2(): lax.ppermute(lax.slice_in_dim(block, block.shape[dim] - width, None, axis...  7.62 us
    concatenate x4, other arithmetic, extended_2(): block = jnp.concatenate([low, block, high], axis=dim)  6 us
    concatenate x3, other arithmetic, local(): extended = jnp.concatenate([past_rows, hidden_pad], 0)  5.66 us
  transfers between devices with their start and end apart: 7, of which 4 were waited for; matrix products, arithmetic and copies ran while one was open for 35% of the time, Pallas kernels for 0%

profile of v1, /device:TPU:125, one launch (start us, length us, event | category | flops | bytes accessed | tf_op | source)
XLA Modules:
  0.0 179.6 jit_solution(8212188231092729876)
XLA Ops:
  24.3 8.0 %all-to-all-start = ((bf16[16,1,1,4,16,512]{5,4,3,2,1,0:T(8,128)(2,1)}), bf16[16,1,1,4,16,512]{5,4,3,2,1,0:T(8,128)(2,1)S(1)}, u32[]{:S(2)}, u32[]{:S(2)}) async-start(bf16[16,1,1,4,16,512]{5,4,3,2,1,0:T(8,128)(2,1)} %fusion.258), calls=%async_computation | async-start | bytes 2097152 | tf_op jit(solution)/shard_map/all_to_all | solution.py:53
  33.4 4.5 %collective-permute-start.3 = (bf16[16,4,1,256]{3,2,1,0:T(2,128)(2,1)S(1)}, bf16[16,4,1,256]{3,2,1,0:T(2,128)(2,1)S(1)}, u32[]{:S(2)}, u32[]{:S(2)}) collective-permute-start(bf16[16,4,1,256]{3,2,1,0:T(2,128)(2,1)S(1)} %get-tuple-element.62), channel_id=1, source_target_pairs={{0,1},{1,2},{2,3},{3,4},{4,5},{5,6},{6,7},{7,8},{8,9},{9,10},{10,1... | collective-permute-start | bytes 98312 | tf_op jit(solution)/shard_map/ppermute | solution.py:14
  37.9 1.9 %collective-permute-start.4 = (bf16[16,4,1,256]{3,2,1,0:T(2,128)(2,1)S(1)}, bf16[16,4,1,256]{3,2,1,0:T(2,128)(2,1)S(1)}, u32[]{:S(2)}, u32[]{:S(2)}) collective-permute-start(bf16[16,4,1,256]{3,2,1,0:T(2,128)(2,1)S(1)} %get-tuple-element.63), channel_id=1, source_target_pairs={{1,0},{2,1},{3,2},{4,3},{5,4},{6,5},{7,6},{8,7},{9,8},{10,9},{11,1... | collective-permute-start | bytes 98312 | tf_op jit(solution)/shard_map/ppermute | solution.py:17
  41.6 14.5 %collective-permute-done.3 = bf16[16,4,1,256]{3,2,1,0:T(2,128)(2,1)S(1)} collective-permute-done((bf16[16,4,1,256]{3,2,1,0:T(2,128)(2,1)S(1)}, bf16[16,4,1,256]{3,2,1,0:T(2,128)(2,1)S(1)}, u32[]{:S(2)}, u32[]{:S(2)}) %collective-permute-start.3) | collective-permute-done | bytes 32800 | tf_op jit(solution)/shard_map/ppermute | solution.py:14
  56.1 2.8 %collective-permute-done.4 = bf16[16,4,1,256]{3,2,1,0:T(2,128)(2,1)S(1)} collective-permute-done((bf16[16,4,1,256]{3,2,1,0:T(2,128)(2,1)S(1)}, bf16[16,4,1,256]{3,2,1,0:T(2,128)(2,1)S(1)}, u32[]{:S(2)}, u32[]{:S(2)}) %collective-permute-start.4) | collective-permute-done | bytes 32800 | tf_op jit(solution)/shard_map/ppermute | solution.py:17
  60.8 2.4 %collective-permute-start.5 = (bf16[2,6,18,256]{3,2,1,0:T(8,128)(2,1)S(1)}, bf16[2,6,18,256]{3,2,1,0:T(8,128)(2,1)S(1)}, u32[]{:S(2)}, u32[]{:S(2)}) collective-permute-start(bf16[2,6,18,256]{3,2,1,0:T(8,128)(2,1)S(1)} %slice.424), channel_id=1, source_target_pairs={{16,0},{17,1},{18,2},{19,3},{20,4},{21,5},{22,6},{23,7},{24,8},{25... | collective-permute-start | bytes 331784 | tf_op jit(solution)/shard_map/ppermute | solution.py:25
  68.1 1.8 %fusion.118 = f32[1024,512]{1,0:T(8,128)} fusion(bf16[1024,256]{1,0:T(8,128)(2,1)S(1)} %bitcast.461, bf16[3,3,3,512,256]{4,3,2,1,0:T(8,128)(2,1)S(1)} %copy-done.2), kind=kOutput, calls=%fused_computation.169 | convolution fusion | flops 268435456 | bytes 2883584 | tf_op jit(solution)/shard_map/dot_general | solution.py:93
  71.1 1.9 %fusion.122 = f32[1024,512]{1,0:T(8,128)} fusion(bf16[1024,256]{1,0:T(8,128)(2,1)S(1)} %bitcast.460, bf16[3,3,3,512,256]{4,3,2,1,0:T(8,128)(2,1)S(1)} %copy-done.2), kind=kOutput, calls=%fused_computation.173 | convolution fusion | flops 268435456 | bytes 2883584 | tf_op jit(solution)/shard_map/dot_general | solution.py:93
  73.0 1.9 %fusion.126 = f32[1024,512]{1,0:T(8,128)} fusion(bf16[1024,256]{1,0:T(8,128)(2,1)S(1)} %bitcast.459, bf16[3,3,3,512,256]{4,3,2,1,0:T(8,128)(2,1)S(1)} %copy-done.2), kind=kOutput, calls=%fused_computation.177 | convolution fusion | flops 268435456 | bytes 2883584 | tf_op jit(solution)/shard_map/dot_general | solution.py:93
  83.8 1.9 %fusion.154 = f32[1024,512]{1,0:T(8,128)} fusion(bf16[1024,256]{1,0:T(8,128)(2,1)S(1)} %bitcast.453, bf16[3,3,3,512,256]{4,3,2,1,0:T(8,128)(2,1)S(1)} %copy-done.2), kind=kOutput, calls=%fused_computation.205 | convolution fusion | flops 268435456 | bytes 2883584 | tf_op jit(solution)/shard_map/dot_general | solution.py:93
  90.7 1.9 %fusion.158 = f32[1024,512]{1,0:T(8,128)} fusion(bf16[1024,256]{1,0:T(8,128)(2,1)S(1)} %bitcast.475, bf16[3,3,3,512,256]{4,3,2,1,0:T(8,128)(2,1)S(1)} %copy-done.2), kind=kOutput, calls=%fused_computation.209 | convolution fusion | flops 268435456 | bytes 2883584 | tf_op jit(solution)/shard_map/dot_general | solution.py:93
  99.7 1.8 %fusion.178 = f32[1024,512]{1,0:T(8,128)} fusion(bf16[1024,256]{1,0:T(8,128)(2,1)S(1)} %bitcast.470, bf16[3,3,3,512,256]{4,3,2,1,0:T(8,128)(2,1)S(1)} %copy-done.2), kind=kOutput, calls=%fused_computation.229 | convolution fusion | flops 268435456 | bytes 2883584 | tf_op jit(solution)/shard_map/dot_general | solution.py:93
  103.3 1.8 %fusion.186 = f32[1024,512]{1,0:T(8,128)} fusion(bf16[1024,256]{1,0:T(8,128)(2,1)S(1)} %bitcast.468, bf16[3,3,3,512,256]{4,3,2,1,0:T(8,128)(2,1)S(1)} %copy-done.2), kind=kOutput, calls=%fused_computation.237 | convolution fusion | flops 268435456 | bytes 2883584 | tf_op jit(solution)/shard_map/dot_general | solution.py:93
  105.1 1.8 %fusion.190 = f32[1024,512]{1,0:T(8,128)} fusion(bf16[1024,256]{1,0:T(8,128)(2,1)S(1)} %bitcast.467, bf16[3,3,3,512,256]{4,3,2,1,0:T(8,128)(2,1)S(1)} %copy-done.2), kind=kOutput, calls=%fused_computation.241 | convolution fusion | flops 268435456 | bytes 2883584 | tf_op jit(solution)/shard_map/dot_general | solution.py:93
  112.7 19.4 %multiply_reduce_fusion = (f32[1024]{0:T(1024)S(1)}, f32[1024,512]{1,0:T(8,128)}) fusion(f32[512]{0:T(512)S(1)} %copy-done.7, f32[1024]{0:T(1024)S(1)} %rsqrt.13, bf16[16,1,1,4,16,512]{5,4,3,2,1,0:T(8,128)(2,1)S(1)} %all-to-all-done, f32[1024,512]{1,0:T(8,128)} %fusion.100, f32[1024,512]{1,0:T(8,128)} %fusion.104, f32[1024,512]{1,0:T(8,128)} %fusion.108, ...), kind=kOutput, calls=%fused_computation.74 | convolution fusion | flops 289405952 | bytes 58468352 | tf_op jit(solution)/shard_map/dot_general | solution.py:93
  133.1 3.1 %collective-permute-start = (bf16[16,4,1,512]{3,2,1,0:T(2,128)(2,1)S(1)}, bf16[16,4,1,512]{3,2,1,0:T(2,128)(2,1)S(1)}, u32[]{:S(2)}, u32[]{:S(2)}) collective-permute-start(bf16[16,4,1,512]{3,2,1,0:T(2,128)(2,1)S(1)} %get-tuple-element.58), channel_id=1, source_target_pairs={{0,1},{1,2},{2,3},{3,4},{4,5},{5,6},{6,7},{7,8},{8,9},{9,10},{10,1... | collective-permute-start | bytes 196616 | tf_op jit(solution)/shard_map/ppermute | solution.py:14
  136.2 1.9 %collective-permute-start.1 = (bf16[16,4,1,512]{3,2,1,0:T(2,128)(2,1)S(1)}, bf16[16,4,1,512]{3,2,1,0:T(2,128)(2,1)S(1)}, u32[]{:S(2)}, u32[]{:S(2)}) collective-permute-start(bf16[16,4,1,512]{3,2,1,0:T(2,128)(2,1)S(1)} %get-tuple-element.59), channel_id=1, source_target_pairs={{1,0},{2,1},{3,2},{4,3},{5,4},{6,5},{7,6},{8,7},{9,8},{10,9},{11,1... | collective-permute-start | bytes 196616 | tf_op jit(solution)/shard_map/ppermute | solution.py:17
  140.3 2.4 %fusion.34 = bf16[16,1,4,16,512]{4,3,2,1,0:T(8,128)(2,1)} fusion(f32[16,4,16,512]{3,2,1,0:T(8,128)S(1)} %bitcast.452, bf16[16,1,1,4,16,512]{5,4,3,2,1,0:T(8,128)(2,1)S(1)} %all-to-all-done, f32[16,4,16]{2,1,0:T(4,128)S(1)} %div.25, f32[512]{0:T(512)S(1)} %copy-done.7, f32[16,4,16]{2,1,0:T(4,128)S(1)} %add_rsqrt_fusion, bf16[512,256]{1,0:T(8,128)(2,1)S(1)} %copy-done, ...), kind=kOutput, calls=%fused_computation.76 | convolution fusion | flops 277348352 | bytes 4990976 | tf_op jit(solution)/shard_map/dot_general | solution.py:81
  146.6 2.1 %pad_maximum_fusion = (bf16[16,4,16,512]{3,2,1,0:T(8,128)(2,1)}, bf16[16,4,16,512]{3,2,1,0:T(8,128)(2,1)S(1)}) fusion(bf16[16,4,1,512]{3,2,1,0:T(2,128)(2,1)S(1)} %collective-permute-done.1, bf16[16,4,16,512]{3,2,1,0:T(8,128)(2,1)S(1)} %fusion.17, bf16[16,4,1,512]{3,2,1,0:T(2,128)(2,1)S(1)} %collective-permute-done), kind=kLoop, calls=%fused_computation.127 | loop fusion | flops 4194304 | bytes 3276800 | tf_op jit(solution)/shard_map/concatenate | solution.py:18
  151.0 4.5 %collective-permute-done.2 = bf16[2,6,18,512]{3,2,1,0:T(8,128)(2,1)S(1)} collective-permute-done((bf16[2,6,18,512]{3,2,1,0:T(8,128)(2,1)S(1)}, bf16[2,6,18,512]{3,2,1,0:T(8,128)(2,1)S(1)}, u32[]{:S(2)}, u32[]{:S(2)}) %collective-permute-start.2) | collective-permute-done | bytes 221216 | tf_op jit(solution)/shard_map/ppermute | solution.py:25
  155.5 2.1 %fusion.78 = (bf16[16,4,16,512]{3,2,1,0:T(8,128)(2,1)S(1)}, bf16[16,4,16,512]{3,2,1,0:T(8,128)(2,1)S(1)}, bf16[16,4,16,512]{3,2,1,0:T(8,128)(2,1)S(1)}, bf16[16,...) fusion(bf16[2,6,18,512]{3,2,1,0:T(8,128)(2,1)S(1)} %collective-, ...), kind=kLoop, calls=%fused_computation.123 | loop fusion | flops 12582912 | bytes 13139968 | tf_op jit(solution)/shard_map/concatenate | solution.py:62
  165.0 2.3 %fusion.67 = (bf16[16,4,16,512]{3,2,1,0:T(8,128)(2,1)}, bf16[16,4,16,512]{3,2,1,0:T(8,128)(2,1)S(1)}, bf16[16,4,16,512]{3,2,1,0:T(8,128)(2,1)S(1)}, bf16[16,4,16...) fusion(bf16[2,6,18,512]{3,2,1,0:T(8,128)(2,1)S(1)} %collective-, ...), kind=kLoop, calls=%fused_computation.112 | loop fusion | flops 3145728 | bytes 11042816 | tf_op jit(solution)/shard_map/concatenate | solution.py:62
  172.4 3.5 %fusion.61 = f32[1024,256]{1,0:T(8,128)} fusion(f32[1024,256]{1,0:T(8,128)S(1)} %fusion.116, f32[1024,256]{1,0:T(8,128)S(1)} %fusion.120, f32[1024,256]{1,0:T(8,128)S(1)} %fusion.124, f32[1024,256]{1,0:T(8,128)S(1)} %fusion.128, f32[1024,256]{1,0:T(8,128)S(1)} %fusion.132, f32[1024,256]{1,0:T(8,128)S(1)} %fusion.136, f32[1024,256]{1,0:T(8,128)S(1)} %fusion.140, ...), kind=kOutput, calls=%fused_computation.106 | convolution fusion | flops 274202624 | bytes 25427968 | tf_op jit(solution)/shard_map/dot_general | solution.py:70
  175.8 3.8 %fusion.62 = bf16[1024,256]{1,0:T(8,128)(2,1)} fusion(f32[1024,256]{1,0:T(8,128)} %fusion.102, f32[1024,256]{1,0:T(8,128)} %fusion.106, f32[1024,256]{1,0:T(8,128)} %fusion.110, f32[1024,256]{1,0:T(8,128)} %fusion.61, bf16[1024,512]{1,0:T(8,128)(2,1)} %bitcast.434, bf16[3,3,3,512,256]{4,3,2,1,0:T(8,128)(2,1)S(1)} %bitcast.419), kind=kOutput, calls=%fused_computation.107 | convolution fusion | flops 269746176 | bytes 6029312 | tf_op jit(solution)/shard_map/dot_general | solution.py:70
  (106 shorter events, 84.6 us)
Async XLA Ops:
  0.6 137.5 %copy-start = (bf16[512,256]{1,0:T(8,128)(2,1)S(1)}, bf16[512,256]{1,0:T(8,128)(2,1)}, u32[]{:S(2)}) copy-start(bf16[512,256]{1,0:T(8,128)(2,1)} %param.8) | copy-start | bytes 786436
  24.3 88.1 %all-to-all-start = ((bf16[16,1,1,4,16,512]{5,4,3,2,1,0:T(8,128)(2,1)}), bf16[16,1,1,4,16,512]{5,4,3,2,1,0:T(8,128)(2,1)S(1)}, u32[]{:S(2)}, u32[]{:S(2)}) async-start(bf16[16,1,1,4,16,512]{5,4,3,2,1,0:T(8,128)(2,1)} %fusion.258), calls=%async_computation | async-start | bytes 2097152 | tf_op jit(solution)/shard_map/all_to_all | solution.py:53
  33.4 22.7 %collective-permute-start.3 = (bf16[16,4,1,256]{3,2,1,0:T(2,128)(2,1)S(1)}, bf16[16,4,1,256]{3,2,1,0:T(2,128)(2,1)S(1)}, u32[]{:S(2)}, u32[]{:S(2)}) collective-permute-start(bf16[16,4,1,256]{3,2,1,0:T(2,128)(2,1)S(1)} %get-tuple-element.62), channel_id=1, source_target_pairs={{0,1},{1,2},{2,3},{3,4},{4,5},{5,6},{6,7},{7,8},{8,9},{9,10},{10,1... | collective-permute-start | bytes 98312 | tf_op jit(solution)/shard_map/ppermute | solution.py:14
  37.9 21.0 %collective-permute-start.4 = (bf16[16,4,1,256]{3,2,1,0:T(2,128)(2,1)S(1)}, bf16[16,4,1,256]{3,2,1,0:T(2,128)(2,1)S(1)}, u32[]{:S(2)}, u32[]{:S(2)}) collective-permute-start(bf16[16,4,1,256]{3,2,1,0:T(2,128)(2,1)S(1)} %get-tuple-element.63), channel_id=1, source_target_pairs={{1,0},{2,1},{3,2},{4,3},{5,4},{6,5},{7,6},{8,7},{9,8},{10,9},{11,1... | collective-permute-start | bytes 98312 | tf_op jit(solution)/shard_map/ppermute | solution.py:17
  39.9 23.3 %copy-start.2 = (bf16[3,3,3,512,256]{4,3,2,1,0:T(8,128)(2,1)S(1)}, bf16[3,3,3,512,256]{4,3,2,1,0:T(8,128)(2,1)}, u32[]{:S(2)}) copy-start(bf16[3,3,3,512,256]{4,3,2,1,0:T(8,128)(2,1)} %param.7) | copy-start | bytes 21233668
  60.8 9.1 %collective-permute-start.5 = (bf16[2,6,18,256]{3,2,1,0:T(8,128)(2,1)S(1)}, bf16[2,6,18,256]{3,2,1,0:T(8,128)(2,1)S(1)}, u32[]{:S(2)}, u32[]{:S(2)}) collective-permute-start(bf16[2,6,18,256]{3,2,1,0:T(8,128)(2,1)S(1)} %slice.424), channel_id=1, source_target_pairs={{16,0},{17,1},{18,2},{19,3},{20,4},{21,5},{22,6},{23,7},{24,8},{25... | collective-permute-start | bytes 331784 | tf_op jit(solution)/shard_map/ppermute | solution.py:25
  65.0 1.8 %copy-start.3 = (bf16[16,1,4,16,256]{4,3,2,1,0:T(8,128)(2,1)S(1)}, bf16[16,1,4,16,256]{4,3,2,1,0:T(8,128)(2,1)}, u32[]{:S(2)}) copy-start(bf16[16,1,4,16,256]{4,3,2,1,0:T(8,128)(2,1)} %param.9) | copy-start | bytes 1572868
  110.5 2.2 %copy-start.7 = (f32[512]{0:T(512)S(1)}, f32[512]{0:T(512)}, u32[]{:S(2)}) copy-start(f32[512]{0:T(512)} %param.6) | copy-start | bytes 6148
  133.1 10.3 %collective-permute-start = (bf16[16,4,1,512]{3,2,1,0:T(2,128)(2,1)S(1)}, bf16[16,4,1,512]{3,2,1,0:T(2,128)(2,1)S(1)}, u32[]{:S(2)}, u32[]{:S(2)}) collective-permute-start(bf16[16,4,1,512]{3,2,1,0:T(2,128)(2,1)S(1)} %get-tuple-element.58), channel_id=1, source_target_pairs={{0,1},{1,2},{2,3},{3,4},{4,5},{5,6},{6,7},{7,8},{8,9},{9,10},{10,1... | collective-permute-start | bytes 196616 | tf_op jit(solution)/shard_map/ppermute | solution.py:14
  136.2 7.5 %collective-permute-start.1 = (bf16[16,4,1,512]{3,2,1,0:T(2,128)(2,1)S(1)}, bf16[16,4,1,512]{3,2,1,0:T(2,128)(2,1)S(1)}, u32[]{:S(2)}, u32[]{:S(2)}) collective-permute-start(bf16[16,4,1,512]{3,2,1,0:T(2,128)(2,1)S(1)} %get-tuple-element.59), channel_id=1, source_target_pairs={{1,0},{2,1},{3,2},{4,3},{5,4},{6,5},{7,6},{8,7},{9,8},{10,9},{11,1... | collective-permute-start | bytes 196616 | tf_op jit(solution)/shard_map/ppermute | solution.py:17
  138.1 2.1 %copy-start.4 = (bf16[16,1,4,16,256]{4,3,2,1,0:T(8,128)(2,1)S(1)}, bf16[16,1,4,16,256]{4,3,2,1,0:T(8,128)(2,1)}, u32[]{:S(2)}) copy-start(bf16[16,1,4,16,256]{4,3,2,1,0:T(8,128)(2,1)} %param.9) | copy-start | bytes 1572868
  138.1 2.1 %copy-start.6 = (f32[1024,512]{1,0:T(8,128)S(1)}, f32[1024,512]{1,0:T(8,128)}, u32[]{:S(2)}) copy-start(f32[1024,512]{1,0:T(8,128)} %get-tuple-element.65) | copy-start | bytes 6291460
  139.6 3.1 %slice-start = ((s8[7077888]{0:T(1024)(128)(4,1)}), s8[4194304]{0:T(1024)(128)(4,1)S(1)}, s32[]{:S(2)}) async-start(s8[7077888]{0:T(1024)(128)(4,1)} %bitcast.418), calls=%async_computation.1 | async-start | bytes 8388608
  140.3 2.7 %slice-start.1 = ((s8[7077888]{0:T(1024)(128)(4,1)}), s8[2883584]{0:T(1024)(128)(4,1)S(1)}, s32[]{:S(2)}) async-start(s8[7077888]{0:T(1024)(128)(4,1)} %bitcast.418), calls=%async_computation.2 | async-start | bytes 5767168
  145.3 10.2 %collective-permute-start.2 = (bf16[2,6,18,512]{3,2,1,0:T(8,128)(2,1)S(1)}, bf16[2,6,18,512]{3,2,1,0:T(8,128)(2,1)S(1)}, u32[]{:S(2)}, u32[]{:S(2)}) collective-permute-start(bf16[2,6,18,512]{3,2,1,0:T(8,128)(2,1)S(1)} %slice.381), channel_id=1, source_target_pairs={{0,16},{1,17},{2,18},{3,19},{4,20},{5,21},{6,22},{7,23},{8,24},{9,... | collective-permute-start | bytes 663560 | tf_op jit(solution)/shard_map/ppermute | solution.py:25
  169.1 2.8 %copy-start.5 = (f32[1024,256]{1,0:T(8,128)S(1)}, f32[1024,256]{1,0:T(8,128)}, u32[]{:S(2)}) copy-start(f32[1024,256]{1,0:T(8,128)} %fusion.279) | copy-start | bytes 3145732
  175.8 3.8 %copy-start.1 = (bf16[512,256]{1,0:T(8,128)(2,1)S(1)}, bf16[512,256]{1,0:T(8,128)(2,1)}, u32[]{:S(2)}) copy-start(bf16[512,256]{1,0:T(8,128)(2,1)} %param.8) | copy-start | bytes 786436
